TPU v7x, 32 devices: a whole 2x2x4 slice. The times are simulated.
32 devices in a mesh: grp: 4 (over y, core), tile: 8 (over z, x).
Axes of the slice: x: 2, y: 2, z: 4, core: 2. Of those that a mesh axis runs over, the one named last changes fastest.
Arguments:
- adjoint_state: float32 [64, 128, 2048], P('tile', 'grp'), may hold values from -6 to 6
- misfit: float32 [64, 128, 2048], P('tile', 'grp'), may hold values from -4 to 4
- east_speed: float32 [64, 128, 2048], P('tile', 'grp'), may hold values from -0.6 to 0.6
- north_speed: float32 [64, 128, 2048], P('tile', 'grp'), may hold values from -0.6 to 0.6
- land_mask: int32 [64, 128, 2048], P('tile', 'grp'), may hold values 0 or 1
- warming_forcing_selector: int32 [128, 2048], P('grp', 'tile'), may hold values 0 or 1
- vertical_filter_matrix: float32 [64, 64], replicated, may hold values from 0 to 0.54
Outputs:
- filtered_thermal_sensitivity: float32 [64, 128, 2048], P('tile', 'grp')
- boundary_warming_sensitivity: float32 [128, 2048], P('grp', 'tile')
All inputs are finite; a program needn't handle non-finite values. No bound on the sum of `land_mask` or of `warming_forcing_selector` on one device may be relied on, other than what follows from the above.
Results may differ from a plain program's by a relative error of at most 0.000088.
Values sent between devices are 32-bit elements; how exact they have to be, the bound alone decides.
A program may use at most 192 MiB of HBM per device.

v0:
```python
import jax
import jax.numpy as jnp
from jax import lax
from jax.sharding import PartitionSpec as P

STEPS = 2


def with_halo(cells, sides, width):
    for axis, dim in sides:
        count = lax.axis_size(axis)
        ends = count - 1
        head = lax.slice_in_dim(cells, 0, width, axis=dim)
        tail = lax.slice_in_dim(cells, cells.shape[dim] - width, cells.shape[dim], axis=dim)
        cells = jnp.concatenate(
            [
                lax.ppermute(tail, axis, [(i, (i + 1) % count) for i in range(ends)]),
                cells,
                lax.ppermute(head, axis, [((i + 1) % count, i) for i in range(ends)]),
            ],
            axis=dim,
        )
    return cells


def advance(padded, misfit, east_speed, north_speed, wet_cells):
    center = padded[1:-1, 1:-1, 1:-1]
    east_cell = padded[1:-1, 1:-1, 2:]
    western_neighbour = padded[1:-1, 1:-1, :-2]
    north_cell = padded[1:-1, 2:, 1:-1]
    south_cell = padded[1:-1, :-2, 1:-1]
    upper_cell = padded[:-2, 1:-1, 1:-1]
    lower_cell = padded[2:, 1:-1, 1:-1]
    vertical = upper_cell + lower_cell - 2.0 * center
    lateral = east_cell + western_neighbour + north_cell + south_cell - 4.0 * center
    change = 0.5 * east_speed * (east_cell - western_neighbour) + 0.5 * north_speed * (
        north_cell - south_cell
    )
    return wet_cells * (center + misfit + change + 0.1 * lateral + 0.15 * vertical)


def smooth_levels(vertical_filter_matrix, pencil):
    return jnp.einsum(
        "cz,zne->cne", vertical_filter_matrix, pencil, precision=lax.Precision.HIGHEST
    )


def body(
    adjoint_state,
    misfit,
    east_speed,
    north_speed,
    land_mask,
    warming_forcing_selector,
    vertical_filter_matrix,
):
    wet_cells = land_mask.astype(jnp.float32)
    current_tracer_values = adjoint_state
    for step_index in range(STEPS):
        bordered = with_halo(current_tracer_values, (("grp", 1), ("tile", 0)), 1)
        padded = jnp.pad(bordered, ((0, 0), (0, 0), (1, 1)))
        current_tracer_values = advance(padded, misfit, east_speed, north_speed, wet_cells)
    pencil = lax.all_to_all(current_tracer_values, "tile", split_axis=2, concat_axis=0, tiled=True)
    smoothed_field = smooth_levels(vertical_filter_matrix, pencil)
    surface_layer = smoothed_field[0]
    filtered_thermal_sensitivity = lax.all_to_all(
        smoothed_field, "tile", split_axis=0, concat_axis=2, tiled=True
    )
    boundary_warming_sensitivity = warming_forcing_selector.astype(jnp.float32) * surface_layer
    return (filtered_thermal_sensitivity, boundary_warming_sensitivity)


def solution(mesh):
    in_specs = (
        P("tile", "grp", None),
        P("tile", "grp", None),
        P("tile", "grp", None),
        P("tile", "grp", None),
        P("tile", "grp", None),
        P("grp", "tile"),
        P(),
    )
    out_specs = (P("tile", "grp", None), P("grp", "tile"))
    return jax.shard_map(body, mesh=mesh, in_specs=in_specs, out_specs=out_specs, check_vma=False)
```

profile of v0, /device:TPU:0, one launch (start us, length us, event | category | flops | bytes accessed | tf_op | source)
XLA Modules:
  0.0 217.6 jit_solution(6359021577452492257)
XLA Ops:
  2.1 2.4 %collective-permute-start = (f32[8,1,2048]{2,0,1:T(8,128)S(1)}, f32[8,1,2048]{2,0,1:T(8,128)S(1)}, u32[]{:S(2)}, u32[]{:S(2)}) collective-permute-start(f32[8,1,2048]{2,0,1:T(8,128)S(1)} %copy.101), channel_id=1, source_target_pairs={{0,8},{8,16},{16,24},{1,9},{9,17},{17,25},{2,10},{10,18},{18,26},{... | collective-permute-start | bytes 196616 | tf_op jit(solution)/shard_map/ppermute | solution.py:17
  5.9 3.9 %collective-permute-done.1 = f32[8,1,2048]{2,0,1:T(8,128)S(1)} collective-permute-done((f32[8,1,2048]{2,0,1:T(8,128)S(1)}, f32[8,1,2048]{2,0,1:T(8,128)S(1)}, u32[]{:S(2)}, u32[]{:S(2)}) %collective-permute-start.1) | collective-permute-done | bytes 65568 | tf_op jit(solution)/shard_map/ppermute | solution.py:19
  11.0 3.4 %collective-permute-start.2 = (f32[1,34,2048]{2,1,0:T(8,128)S(1)}, f32[1,34,2048]{2,1,0:T(8,128)S(1)}, u32[]{:S(2)}, u32[]{:S(2)}) collective-permute-start(f32[1,34,2048]{2,1,0:T(8,128)S(1)} %get-tuple-element.4), channel_id=1, source_target_pairs={{0,1},{1,2},{2,3},{3,4},{4,5},{5,6},{6,7},{8,9},{9,10},{10,11},{11... | collective-permute-start | bytes 835592 | tf_op jit(solution)/shard_map/ppermute | solution.py:17
  16.0 4.3 %collective-permute-done.2 = f32[1,34,2048]{2,1,0:T(8,128)S(1)} collective-permute-done((f32[1,34,2048]{2,1,0:T(8,128)S(1)}, f32[1,34,2048]{2,1,0:T(8,128)S(1)}, u32[]{:S(2)}, u32[]{:S(2)}) %collective-permute-start.2) | collective-permute-done | bytes 278560 | tf_op jit(solution)/shard_map/ppermute | solution.py:17
  20.3 5.0 %collective-permute-done.3 = f32[1,34,2048]{2,1,0:T(8,128)S(1)} collective-permute-done((f32[1,34,2048]{2,1,0:T(8,128)S(1)}, f32[1,34,2048]{2,1,0:T(8,128)S(1)}, u32[]{:S(2)}, u32[]{:S(2)}) %collective-permute-start.3) | collective-permute-done | bytes 278560 | tf_op jit(solution)/shard_map/ppermute | solution.py:19
  25.3 3.1 %select_maximum_fusion.4 = f32[10,34,2050]{2,1,0:T(8,128)S(1)} fusion(f32[1,34,2048]{2,1,0:T(8,128)S(1)} %collective-permute-done.3, f32[1,34,2048]{2,1,0:T(8,128)S(1)} %collective-permute-done.2, f32[8,1,2048]{2,1,0:T(1,128)S(1)} %copy.87, f32[8,32,2048]{2,1,0:T(8,128)S(1)} %copy-done.1, f32[8,1,2048]{2,1,0:T(1,128)S(1)} %copy.86), kind=kLoop, calls=%fused_computation.6 | loop fusion | flops 8364000 | bytes 5573280 | tf_op jit(solution)/shard_map/concatenate | solution.py:15
  28.5 4.3 %fusion.10 = f32[8,32,2048]{2,1,0:T(8,128)S(1)} fusion(f32[1,34,2048]{2,1,0:T(8,128)S(1)} %collective-permute-done.3, f32[8,1,2048]{2,1,0:T(1,128)S(1)} %copy.87, f32[8,32,2048]{2,1,0:T(8,128)S(1)} %copy-done.1, f32[8,1,2048]{2,1,0:T(1,128)S(1)} %copy.86, f32[1,34,2048]{2,1,0:T(8,128)S(1)} %collective-permute-done.2, ...), kind=kLoop, calls=%fused_computation.29 | loop fusion | flops 16252928 | bytes 17465344 | tf_op jit(solution)/shard_map/mul | solution.py:39
  32.9 6.2 %collective-permute-start.4 = (f32[8,1,2048]{2,0,1:T(8,128)S(1)}, f32[8,1,2048]{2,0,1:T(8,128)S(1)}, u32[]{:S(2)}, u32[]{:S(2)}) collective-permute-start(f32[8,1,2048]{2,0,1:T(8,128)S(1)} %copy.90), channel_id=1, source_target_pairs={{0,8},{8,16},{16,24},{1,9},{9,17},{17,25},{2,10},{10,18},{18,26},{... | collective-permute-start | bytes 196616 | tf_op jit(solution)/shard_map/ppermute | solution.py:17
  42.5 4.1 %collective-permute-start.6 = (f32[1,34,2048]{2,1,0:T(8,128)S(1)}, f32[1,34,2048]{2,1,0:T(8,128)S(1)}, u32[]{:S(2)}, u32[]{:S(2)}) collective-permute-start(f32[1,34,2048]{2,1,0:T(8,128)S(1)} %get-tuple-element.2), channel_id=1, source_target_pairs={{0,1},{1,2},{2,3},{3,4},{4,5},{5,6},{6,7},{8,9},{9,10},{10,11},{11... | collective-permute-start | bytes 835592 | tf_op jit(solution)/shard_map/ppermute | solution.py:17
  48.0 5.1 %collective-permute-done.6 = f32[1,34,2048]{2,1,0:T(8,128)S(1)} collective-permute-done((f32[1,34,2048]{2,1,0:T(8,128)S(1)}, f32[1,34,2048]{2,1,0:T(8,128)S(1)}, u32[]{:S(2)}, u32[]{:S(2)}) %collective-permute-start.6) | collective-permute-done | bytes 278560 | tf_op jit(solution)/shard_map/ppermute | solution.py:17
  53.1 5.2 %collective-permute-done.7 = f32[1,34,2048]{2,1,0:T(8,128)S(1)} collective-permute-done((f32[1,34,2048]{2,1,0:T(8,128)S(1)}, f32[1,34,2048]{2,1,0:T(8,128)S(1)}, u32[]{:S(2)}, u32[]{:S(2)}) %collective-permute-start.7) | collective-permute-done | bytes 278560 | tf_op jit(solution)/shard_map/ppermute | solution.py:19
  58.3 3.1 %select_maximum_fusion = f32[10,34,2050]{2,1,0:T(8,128)S(1)} fusion(f32[1,34,2048]{2,1,0:T(8,128)S(1)} %collective-permute-done.7, f32[1,34,2048]{2,1,0:T(8,128)S(1)} %collective-permute-done.6, f32[8,1,2048]{2,1,0:T(1,128)S(1)} %copy.93, f32[8,32,2048]{2,1,0:T(8,128)S(1)} %fusion.10, f32[8,1,2048]{2,1,0:T(1,128)S(1)} %copy.92), kind=kLoop, calls=%fused_computation.2 | loop fusion | flops 8364000 | bytes 5573280 | tf_op jit(solution)/shard_map/concatenate | solution.py:15
  61.4 3.0 %fusion.5 = f32[8,32,2048]{2,1,0:T(8,128)S(1)} fusion(f32[1,34,2048]{2,1,0:T(8,128)S(1)} %collective-permute-done.7, f32[8,1,2048]{2,1,0:T(1,128)S(1)} %copy.93, f32[8,32,2048]{2,1,0:T(8,128)S(1)} %fusion.10, f32[8,1,2048]{2,1,0:T(1,128)S(1)} %copy.92, f32[1,34,2048]{2,1,0:T(8,128)S(1)} %collective-permute-done.6, ...), kind=kLoop, calls=%fused_computation.16 | loop fusion | flops 16252928 | bytes 17465344 | tf_op jit(solution)/shard_map/mul | solution.py:39
  64.5 4.7 %copy.96 = f32[8,32,2048]{1,0,2:T(8,128)} copy(f32[8,32,2048]{2,1,0:T(8,128)S(1)} %fusion.5) | data formatting | bytes 4194304 | tf_op jit(solution)/shard_map/mul | solution.py:39
  69.2 7.4 %reshape.5 = f32[8,1,65536]{2,1,0:T(1,128)S(1)} reshape(f32[2048,8,32]{2,1,0:T(8,128)} %bitcast.22) | data formatting | bytes 4194304
  76.6 59.5 %all_to_all.36 = f32[8,1,65536]{2,1,0:T(1,128)} all-to-all(f32[8,1,65536]{2,1,0:T(1,128)S(1)} %reshape.5), channel_id=1, replica_groups=mesh['grp'=4,'tile'=8] {'tile'}, dimensions={0} | all-to-all | bytes 4194304 | tf_op jit(solution)/shard_map/all_to_all | solution.py:63
  136.7 7.2 %reduce = f32[8,65536]{1,0:T(8,128)S(1)} reduce(f32[8,1,65536]{2,1,0:T(1,128)} %all_to_all.36, f32[]{:T(128)} %broadcast.70), dimensions={1}, to_apply=%all_to_all.26.reduce_sub_computation | reduce | bytes 4194308 | tf_op jit(solution)/shard_map/all_to_all | solution.py:63
  143.9 6.0 %reshape.6 = f32[2048,8,32]{2,1,0:T(8,128)} reshape(f32[8,65536]{1,0:T(8,128)S(1)} %reduce) | data formatting | bytes 4194304
  149.9 6.6 %copy.97 = f32[8,32,8,256]{3,0,2,1:T(8,128)} copy(f32[8,32,8,256]{1,0,3,2:T(8,128)} %bitcast.23) | data formatting | bytes 4194304 | tf_op jit(solution)/shard_map/all_to_all | solution.py:63
  156.5 3.6 %fusion.13 = f32[64,32,256]{2,0,1:T(8,128)S(1)} fusion(f32[8,32,8,256]{3,0,2,1:T(8,128)} %copy.97, f32[64,64]{1,0:T(8,128)S(1)} %copy-done), kind=kOutput, calls=%fused_computation.39 | convolution fusion | flops 402653184 | bytes 4210688 | tf_op jit(solution)/shard_map/cz,zne->cne/dot_general | solution.py:43
  160.1 2.5 %copy.98 = f32[64,32,256]{2,1,0:T(8,128)} copy(f32[64,32,256]{2,0,1:T(8,128)S(1)} %fusion.13) | data formatting | bytes 4194304 | tf_op jit(solution)/shard_map/cz,zne->cne/dot_general | solution.py:43
  162.6 4.5 %all-to-all-start.1 = ((f32[64,32,256]{2,1,0:T(8,128)}), f32[64,32,256]{2,1,0:T(8,128)}, u32[]{:S(2)}, u32[]{:S(2)}) async-start(f32[64,32,256]{2,1,0:T(8,128)} %copy.98), calls=%async_computation.1 | async-start | bytes 4194304 | tf_op jit(solution)/shard_map/all_to_all | solution.py:66
  167.8 46.7 %all-to-all-done.1 = f32[64,32,256]{2,1,0:T(8,128)} async-done(((f32[64,32,256]{2,1,0:T(8,128)}), f32[64,32,256]{2,1,0:T(8,128)}, u32[]{:S(2)}, u32[]{:S(2)}) %all-to-all-start.1) | async-done | bytes 2097184 | tf_op jit(solution)/shard_map/all_to_all | solution.py:66
  214.4 3.2 %copy.103 = f32[8,8,4,8,256]{4,3,0,2,1:T(8,128)} copy(f32[8,8,4,8,256]{4,3,2,1,0:T(8,128)} %bitcast.10) | data formatting | bytes 4194304 | tf_op jit(solution)/shard_map/all_to_all | solution.py:66
  (36 shorter events, 11.6 us)
Async XLA Ops:
  0.6 155.8 %copy-start = (f32[64,64]{1,0:T(8,128)S(1)}, f32[64,64]{1,0:T(8,128)}, u32[]{:S(2)}) copy-start(f32[64,64]{1,0:T(8,128)} %param.13) | copy-start | bytes 49156
  0.6 24.7 %copy-start.1 = (f32[8,32,2048]{2,1,0:T(8,128)S(1)}, f32[8,32,2048]{2,1,0:T(8,128)}, u32[]{:S(2)}) copy-start(f32[8,32,2048]{2,1,0:T(8,128)} %param.7) | copy-start | bytes 6291460
  2.1 3.7 %collective-permute-start = (f32[8,1,2048]{2,0,1:T(8,128)S(1)}, f32[8,1,2048]{2,0,1:T(8,128)S(1)}, u32[]{:S(2)}, u32[]{:S(2)}) collective-permute-start(f32[8,1,2048]{2,0,1:T(8,128)S(1)} %copy.101), channel_id=1, source_target_pairs={{0,8},{8,16},{16,24},{1,9},{9,17},{17,25},{2,10},{10,18},{18,26},{... | collective-permute-start | bytes 196616 | tf_op jit(solution)/shard_map/ppermute | solution.py:17
  4.5 5.3 %collective-permute-start.1 = (f32[8,1,2048]{2,0,1:T(8,128)S(1)}, f32[8,1,2048]{2,0,1:T(8,128)S(1)}, u32[]{:S(2)}, u32[]{:S(2)}) collective-permute-start(f32[8,1,2048]{2,0,1:T(8,128)S(1)} %copy.102), channel_id=1, source_target_pairs={{8,0},{16,8},{24,16},{9,1},{17,9},{25,17},{10,2},{18,10},{26,18},{... | collective-permute-start | bytes 196616 | tf_op jit(solution)/shard_map/ppermute | solution.py:19
  11.0 9.3 %collective-permute-start.2 = (f32[1,34,2048]{2,1,0:T(8,128)S(1)}, f32[1,34,2048]{2,1,0:T(8,128)S(1)}, u32[]{:S(2)}, u32[]{:S(2)}) collective-permute-start(f32[1,34,2048]{2,1,0:T(8,128)S(1)} %get-tuple-element.4), channel_id=1, source_target_pairs={{0,1},{1,2},{2,3},{3,4},{4,5},{5,6},{6,7},{8,9},{9,10},{10,11},{11... | collective-permute-start | bytes 835592 | tf_op jit(solution)/shard_map/ppermute | solution.py:17
  14.4 14.0 %copy-start.2 = (f32[8,32,2048]{2,1,0:T(8,128)S(1)}, f32[8,32,2048]{2,1,0:T(8,128)}, u32[]{:S(2)}) copy-start(f32[8,32,2048]{2,1,0:T(8,128)} %param.8) | copy-start | bytes 6291460
  14.4 14.0 %copy-start.3 = (s32[8,32,2048]{2,1,0:T(8,128)S(1)}, s32[8,32,2048]{2,1,0:T(8,128)}, u32[]{:S(2)}) copy-start(s32[8,32,2048]{2,1,0:T(8,128)} %param.11) | copy-start | bytes 6291460
  14.5 14.0 %copy-start.4 = (f32[8,32,2048]{2,1,0:T(8,128)S(1)}, f32[8,32,2048]{2,1,0:T(8,128)}, u32[]{:S(2)}) copy-start(f32[8,32,2048]{2,1,0:T(8,128)} %param.10) | copy-start | bytes 6291460
  14.5 10.9 %collective-permute-start.3 = (f32[1,34,2048]{2,1,0:T(8,128)S(1)}, f32[1,34,2048]{2,1,0:T(8,128)S(1)}, u32[]{:S(2)}, u32[]{:S(2)}) collective-permute-start(f32[1,34,2048]{2,1,0:T(8,128)S(1)} %get-tuple-element.5), channel_id=1, source_target_pairs={{1,0},{2,1},{3,2},{4,3},{5,4},{6,5},{7,6},{9,8},{10,9},{11,10},{12... | collective-permute-start | bytes 835592 | tf_op jit(solution)/shard_map/ppermute | solution.py:19
  32.9 7.6 %collective-permute-start.4 = (f32[8,1,2048]{2,0,1:T(8,128)S(1)}, f32[8,1,2048]{2,0,1:T(8,128)S(1)}, u32[]{:S(2)}, u32[]{:S(2)}) collective-permute-start(f32[8,1,2048]{2,0,1:T(8,128)S(1)} %copy.90), channel_id=1, source_target_pairs={{0,8},{8,16},{16,24},{1,9},{9,17},{17,25},{2,10},{10,18},{18,26},{... | collective-permute-start | bytes 196616 | tf_op jit(solution)/shard_map/ppermute | solution.py:17
  39.1 3.1 %collective-permute-start.5 = (f32[8,1,2048]{2,0,1:T(8,128)S(1)}, f32[8,1,2048]{2,0,1:T(8,128)S(1)}, u32[]{:S(2)}, u32[]{:S(2)}) collective-permute-start(f32[8,1,2048]{2,0,1:T(8,128)S(1)} %copy.91), channel_id=1, source_target_pairs={{8,0},{16,8},{24,16},{9,1},{17,9},{25,17},{10,2},{18,10},{26,18},{... | collective-permute-start | bytes 196616 | tf_op jit(solution)/shard_map/ppermute | solution.py:19
  42.5 10.6 %collective-permute-start.6 = (f32[1,34,2048]{2,1,0:T(8,128)S(1)}, f32[1,34,2048]{2,1,0:T(8,128)S(1)}, u32[]{:S(2)}, u32[]{:S(2)}) collective-permute-start(f32[1,34,2048]{2,1,0:T(8,128)S(1)} %get-tuple-element.2), channel_id=1, source_target_pairs={{0,1},{1,2},{2,3},{3,4},{4,5},{5,6},{6,7},{8,9},{9,10},{10,11},{11... | collective-permute-start | bytes 835592 | tf_op jit(solution)/shard_map/ppermute | solution.py:17
  46.6 14.8 %copy-start.5 = (f32[8,32,2048]{2,1,0:T(8,128)S(1)}, f32[8,32,2048]{2,1,0:T(8,128)}, u32[]{:S(2)}) copy-start(f32[8,32,2048]{2,1,0:T(8,128)} %param.9) | copy-start | bytes 6291460
  46.6 11.7 %collective-permute-start.7 = (f32[1,34,2048]{2,1,0:T(8,128)S(1)}, f32[1,34,2048]{2,1,0:T(8,128)S(1)}, u32[]{:S(2)}, u32[]{:S(2)}) collective-permute-start(f32[1,34,2048]{2,1,0:T(8,128)S(1)} %get-tuple-element.3), channel_id=1, source_target_pairs={{1,0},{2,1},{3,2},{4,3},{5,4},{6,5},{7,6},{9,8},{10,9},{11,10},{12... | collective-permute-start | bytes 835592 | tf_op jit(solution)/shard_map/ppermute | solution.py:19
  162.6 4.5 %copy-start.6 = (s32[32,256]{1,0:T(8,128)S(1)}, s32[32,256]{1,0:T(8,128)}, u32[]{:S(2)}) copy-start(s32[32,256]{1,0:T(8,128)} %param.12) | copy-start | bytes 98308
  162.6 51.8 %all-to-all-start.1 = ((f32[64,32,256]{2,1,0:T(8,128)}), f32[64,32,256]{2,1,0:T(8,128)}, u32[]{:S(2)}, u32[]{:S(2)}) async-start(f32[64,32,256]{2,1,0:T(8,128)} %copy.98), calls=%async_computation.1 | async-start | bytes 4194304 | tf_op jit(solution)/shard_map/all_to_all | solution.py:66
where the time goes:
time: 218 us
  waiting for transfers between devices  71.9 us (33%)
  blocking collectives  59.5 us (27%)
  local copies, waits for them, and re-layouts  32.9 us (15%)
  starting transfers between devices  26.2 us (12%)
  other arithmetic  22.6 us (10%)
  matrix products  3.6 us (2%)
    all_to_all x1, blocking collectives, body(): lax.all_to_all(current_tracer_values, 'tile', split_axis=2, concat_axis=0...  59.5 us
    all_to_all x1, waiting for transfers between devices, body(): lax.all_to_all(smoothed_field, 'tile', split_axis=0, concat_axis=2, tiled...  46.7 us
    ppermute x4, starting transfers between devices, with_halo(): lax.ppermute(tail, axis, [(i, (i + 1) % count) for i in range(ends)])  16.1 us
    ppermute x4, waiting for transfers between devices, with_halo(): lax.ppermute(head, axis, [((i + 1) % count, i) for i in range(ends)])  15.8 us
    unnamed x18, local copies, waits for them, and re-layouts  13.5 us
    ppermute x4, waiting for transfers between devices, with_halo(): lax.ppermute(tail, axis, [(i, (i + 1) % count) for i in range(ends)])  9.4 us
    mul x2, other arithmetic, advance(): wet_cells * (center + misfit + change + 0.1 * lateral + 0.15 * vertical)  7.31 us
    all_to_all x1, other arithmetic, body(): lax.all_to_all(current_tracer_values, 'tile', split_axis=2, concat_axis=0...  7.22 us
  transfers between devices with their start and end apart: 9, of which 7 were waited for; matrix products, arithmetic and copies ran while one was open for 0% of the time, Pallas kernels for 0%

commit v1 on v0

--- a/solution.py
+++ b/solution.py
@@ -1,9 +1,31 @@
+import functools
 import jax
 import jax.numpy as jnp
 from jax import lax
 from jax.sharding import PartitionSpec as P
 
 STEPS = 2
+
+
+def detail_types(panel, d_out, dimension_no):
+    lower, val2 = (lax.axis_size("tile"), lax.axis_index("tile"))
+    step_out = panel.shape[d_out] // lower
+    wide_out = list(panel.shape)
+    wide_out[d_out] = step_out
+    high = wide_out[dimension_no]
+    wide_out[dimension_no] = high * lower
+    piece_now = jnp.zeros(wide_out, panel.dtype)
+    for q in range(lower):
+        prior = lax.dynamic_slice_in_dim(panel, (val2 ^ q) * step_out, step_out, axis=d_out)
+        if q:
+            prior = lax.ppermute(prior, "tile", list(map(lambda w: (w, w ^ q), range(lower))))
+        piece_now = lax.dynamic_update_slice_in_dim(
+            piece_now, prior, (val2 ^ q) * high, axis=dimension_no
+        )
+    return piece_now
+
+
+lift_meshes_on_mesh = functools.partial(detail_types, d_out=2, dimension_no=0)
 
 
 def with_halo(cells, sides, width):
@@ -60,7 +82,7 @@
         bordered = with_halo(current_tracer_values, (("grp", 1), ("tile", 0)), 1)
         padded = jnp.pad(bordered, ((0, 0), (0, 0), (1, 1)))
         current_tracer_values = advance(padded, misfit, east_speed, north_speed, wet_cells)
-    pencil = lax.all_to_all(current_tracer_values, "tile", split_axis=2, concat_axis=0, tiled=True)
+    pencil = lift_meshes_on_mesh(current_tracer_values)
     smoothed_field = smooth_levels(vertical_filter_matrix, pencil)
     surface_layer = smoothed_field[0]
     filtered_thermal_sensitivity = lax.all_to_all(

time: 218 us -> 185 us (0.85)
  blocking collectives: 59.5 us -> 0 us
  starting transfers between devices: 26.2 us -> 59 us
  local copies, waits for them, and re-layouts: 32.9 us -> 9.15 us
  waiting for transfers between devices: 71.9 us -> 95.6 us
  other arithmetic: 22.6 us -> 17.3 us
    all_to_all x1 -> x0, blocking collectives: 59.5 us -> none  [body(): lax.all_to_all(current_tracer_values, 'tile', split_axis=2, concat_axis=0...]
    ppermute x0 -> x7, waiting for transfers between devices: none -> 24.2 us  [detail_types(): lax.ppermute(prior, 'tile', list(map(lambda w: (w, w ^ q), range(lower))))]
    ppermute x0 -> x7, starting transfers between devices: none -> 22.7 us  [detail_types(): lax.ppermute(prior, 'tile', list(map(lambda w: (w, w ^ q), range(lower))))]
    unnamed x18, local copies, waits for them, and re-layouts: 13.5 us -> 0.06 us
    all_to_all x1, starting transfers between devices: 4.49 us -> 14.6 us  [body(): lax.all_to_all(smoothed_field, 'tile', split_axis=0, concat_axis=2, tiled...]
    all_to_all x1 -> x0, other arithmetic: 7.22 us -> none  [body(): lax.all_to_all(current_tracer_values, 'tile', split_axis=2, concat_axis=0...]
    all_to_all x2 -> x0, local copies, waits for them, and re-layouts: 7.09 us -> none  [body(): lax.all_to_all(current_tracer_values, 'tile', split_axis=2, concat_axis=0...]
    mul x1 -> x0, local copies, waits for them, and re-layouts: 4.74 us -> none  [advance(): wet_cells * (center + misfit + change + 0.1 * lateral + 0.15 * vertical)]
  transfers between devices with their start and end apart: 9 -> 16, of which waited for: 7 -> 10; matrix products, arithmetic and copies ran while one was open for 0% -> 1% of each run, Pallas kernels for 0% -> 0%
where the time goes in v1:
time: 185 us; the launch traced here: 184 us
  waiting for transfers between devices  95.6 us (52%)
  starting transfers between devices  59 us (32%)
  other arithmetic  17.3 us (9%)
  local copies, waits for them, and re-layouts  9.15 us (5%)
  matrix products  2.01 us (1%)
    all_to_all x1, waiting for transfers between devices, body(): lax.all_to_all(smoothed_field, 'tile', split_axis=0, concat_axis=2, tiled...  46.3 us
    ppermute x7, waiting for transfers between devices, detail_types(): lax.ppermute(prior, 'tile', list(map(lambda w: (w, w ^ q), range(lower))))  24.2 us
    ppermute x7, starting transfers between devices, detail_types(): lax.ppermute(prior, 'tile', list(map(lambda w: (w, w ^ q), range(lower))))  22.7 us
    ppermute x4, starting transfers between devices, with_halo(): lax.ppermute(tail, axis, [(i, (i + 1) % count) for i in range(ends)])  16.1 us
    ppermute x4, waiting for transfers between devices, with_halo(): lax.ppermute(head, axis, [((i + 1) % count, i) for i in range(ends)])  15.5 us
    all_to_all x1, starting transfers between devices, body(): lax.all_to_all(smoothed_field, 'tile', split_axis=0, concat_axis=2, tiled...  14.6 us
    ppermute x4, waiting for transfers between devices, with_halo(): lax.ppermute(tail, axis, [(i, (i + 1) % count) for i in range(ends)])  9.57 us
    mul x2, other arithmetic, advance(): wet_cells * (center + misfit + change + 0.1 * lateral + 0.15 * vertical)  8.52 us
  transfers between devices with their start and end apart: 16, of which 10 were waited for; matrix products, arithmetic and copies ran while one was open for 1% of the time, Pallas kernels for 0%

profile of v1, /device:TPU:0, one launch (start us, length us, event | category | flops | bytes accessed | tf_op | source)
XLA Modules:
  0.0 184.1 jit_solution(6232462803269719294)
XLA Ops:
  2.1 2.4 %collective-permute-start = (f32[8,1,2048]{2,1,0:T(1,128)S(1)}, f32[8,1,2048]{2,1,0:T(1,128)S(1)}, u32[]{:S(2)}, u32[]{:S(2)}) collective-permute-start(f32[8,1,2048]{2,1,0:T(1,128)S(1)} %get-tuple-element.16), channel_id=1, source_target_pairs={{0,8},{8,16},{16,24},{1,9},{9,17},{17,25},{2,10},{10,18},{18,26},{... | collective-permute-start | bytes 196616 | tf_op jit(solution)/shard_map/ppermute | solution.py:39
  5.8 4.0 %collective-permute-done.1 = f32[8,1,2048]{2,1,0:T(1,128)S(1)} collective-permute-done((f32[8,1,2048]{2,1,0:T(1,128)S(1)}, f32[8,1,2048]{2,1,0:T(1,128)S(1)}, u32[]{:S(2)}, u32[]{:S(2)}) %collective-permute-start.1) | collective-permute-done | bytes 65568 | tf_op jit(solution)/shard_map/ppermute | solution.py:41
  10.9 3.4 %collective-permute-start.2 = (f32[1,34,2048]{2,1,0:T(8,128)S(1)}, f32[1,34,2048]{2,1,0:T(8,128)S(1)}, u32[]{:S(2)}, u32[]{:S(2)}) collective-permute-start(f32[1,34,2048]{2,1,0:T(8,128)S(1)} %get-tuple-element.4), channel_id=1, source_target_pairs={{0,1},{1,2},{2,3},{3,4},{4,5},{5,6},{6,7},{8,9},{9,10},{10,11},{11... | collective-permute-start | bytes 835592 | tf_op jit(solution)/shard_map/ppermute | solution.py:39
  15.9 4.3 %collective-permute-done.2 = f32[1,34,2048]{2,1,0:T(8,128)S(1)} collective-permute-done((f32[1,34,2048]{2,1,0:T(8,128)S(1)}, f32[1,34,2048]{2,1,0:T(8,128)S(1)}, u32[]{:S(2)}, u32[]{:S(2)}) %collective-permute-start.2) | collective-permute-done | bytes 278560 | tf_op jit(solution)/shard_map/ppermute | solution.py:39
  20.2 5.0 %collective-permute-done.3 = f32[1,34,2048]{2,1,0:T(8,128)S(1)} collective-permute-done((f32[1,34,2048]{2,1,0:T(8,128)S(1)}, f32[1,34,2048]{2,1,0:T(8,128)S(1)}, u32[]{:S(2)}, u32[]{:S(2)}) %collective-permute-start.3) | collective-permute-done | bytes 278560 | tf_op jit(solution)/shard_map/ppermute | solution.py:41
  25.2 3.1 %select_maximum_fusion.4 = f32[10,34,2050]{2,1,0:T(8,128)S(1)} fusion(f32[1,34,2048]{2,1,0:T(8,128)S(1)} %collective-permute-done.3, f32[1,34,2048]{2,1,0:T(8,128)S(1)} %collective-permute-done.2, f32[8,1,2048]{2,1,0:T(1,128)S(1)} %collective-permute-done.1, f32[8,32,2048]{2,1,0:T(8,128)S(1)} %copy-done.1, f32[8,1,2048]{2,1,0:T(1,128)S(1)} %collective-permute-done), kind=kLoop, calls=%fused_computation.6 | loop fusion | flops 8364000 | bytes 5573280 | tf_op jit(solution)/shard_map/concatenate | solution.py:37
  28.3 4.3 %fusion.10 = f32[8,32,2048]{2,1,0:T(8,128)S(1)} fusion(f32[1,34,2048]{2,1,0:T(8,128)S(1)} %collective-permute-done.3, f32[8,1,2048]{2,1,0:T(1,128)S(1)} %collective-permute-done.1, f32[8,32,2048]{2,1,0:T(8,128)S(1)} %copy-done.1, f32[8,1,2048]{2,1,0:T(1,128)S(1)} %collective-permute-done, f32[1,34,2048]{2,1,0:T(8,128)S(1)} %collective-permute-done.2, ...), kind=kLoop, calls=%fused_computation.29 | loop fusion | flops 16252928 | bytes 17465344 | tf_op jit(solution)/shard_map/mul | solution.py:61
  32.7 6.2 %collective-permute-start.4 = (f32[8,1,2048]{2,1,0:T(1,128)S(1)}, f32[8,1,2048]{2,1,0:T(1,128)S(1)}, u32[]{:S(2)}, u32[]{:S(2)}) collective-permute-start(f32[8,1,2048]{2,1,0:T(1,128)S(1)} %get-tuple-element.14), channel_id=1, source_target_pairs={{0,8},{8,16},{16,24},{1,9},{9,17},{17,25},{2,10},{10,18},{18,26},{... | collective-permute-start | bytes 196616 | tf_op jit(solution)/shard_map/ppermute | solution.py:39
  42.9 4.1 %collective-permute-start.6 = (f32[1,34,2048]{2,1,0:T(8,128)}, f32[1,34,2048]{2,1,0:T(8,128)S(1)}, u32[]{:S(2)}, u32[]{:S(2)}) collective-permute-start(f32[1,34,2048]{2,1,0:T(8,128)} %get-tuple-element.2), channel_id=1, source_target_pairs={{0,1},{1,2},{2,3},{3,4},{4,5},{5,6},{6,7},{8,9},{9,10},{10,11},{11... | collective-permute-start | bytes 835592 | tf_op jit(solution)/shard_map/ppermute | solution.py:39
  48.6 5.3 %collective-permute-done.6 = f32[1,34,2048]{2,1,0:T(8,128)S(1)} collective-permute-done((f32[1,34,2048]{2,1,0:T(8,128)}, f32[1,34,2048]{2,1,0:T(8,128)S(1)}, u32[]{:S(2)}, u32[]{:S(2)}) %collective-permute-start.6) | collective-permute-done | bytes 278560 | tf_op jit(solution)/shard_map/ppermute | solution.py:39
  53.8 4.7 %collective-permute-done.7 = f32[1,34,2048]{2,1,0:T(8,128)S(1)} collective-permute-done((f32[1,34,2048]{2,1,0:T(8,128)S(1)}, f32[1,34,2048]{2,1,0:T(8,128)S(1)}, u32[]{:S(2)}, u32[]{:S(2)}) %collective-permute-start.7) | collective-permute-done | bytes 278560 | tf_op jit(solution)/shard_map/ppermute | solution.py:41
  58.5 3.1 %select_maximum_fusion = f32[10,34,2050]{2,1,0:T(8,128)S(1)} fusion(f32[1,34,2048]{2,1,0:T(8,128)S(1)} %collective-permute-done.7, f32[1,34,2048]{2,1,0:T(8,128)S(1)} %collective-permute-done.6, f32[8,1,2048]{2,1,0:T(1,128)S(1)} %collective-permute-done.5, f32[8,32,2048]{2,1,0:T(8,128)S(1)} %fusion.10, f32[8,1,2048]{2,1,0:T(1,128)S(1)} %collective-permute-done.4), kind=kLoop, calls=%fused_computation.2 | loop fusion | flops 8364000 | bytes 5573280 | tf_op jit(solution)/shard_map/concatenate | solution.py:37
  61.7 4.3 %fusion.5 = f32[8,32,2048]{2,1,0:T(8,128)S(1)} fusion(f32[1,34,2048]{2,1,0:T(8,128)S(1)} %collective-permute-done.7, f32[8,1,2048]{2,1,0:T(1,128)S(1)} %collective-permute-done.5, f32[8,32,2048]{2,1,0:T(8,128)S(1)} %fusion.10, f32[8,1,2048]{2,1,0:T(1,128)S(1)} %collective-permute-done.4, f32[1,34,2048]{2,1,0:T(8,128)S(1)} %collective-permute-done.6, ...), kind=kLoop, calls=%fused_computation.16 | loop fusion | flops 16252928 | bytes 17465344 | tf_op jit(solution)/shard_map/mul | solution.py:61
  66.2 4.8 %collective-permute-start.8 = (f32[8,32,256]{2,1,0:T(8,128)S(1)}, f32[8,32,256]{2,1,0:T(8,128)S(1)}, u32[]{:S(2)}, u32[]{:S(2)}) collective-permute-start(f32[8,32,256]{2,1,0:T(8,128)S(1)} %get-tuple-element.12), channel_id=1, source_target_pairs={{0,1},{1,0},{2,3},{3,2},{4,5},{5,4},{6,7},{7,6},{8,9},{9,8},{10,11... | collective-permute-start | bytes 786440 | tf_op jit(solution)/shard_map/ppermute | solution.py:21
  71.0 3.6 %collective-permute-start.9 = (f32[8,32,256]{2,1,0:T(8,128)S(1)}, f32[8,32,256]{2,1,0:T(8,128)S(1)}, u32[]{:S(2)}, u32[]{:S(2)}) collective-permute-start(f32[8,32,256]{2,1,0:T(8,128)S(1)} %get-tuple-element.11), channel_id=1, source_target_pairs={{0,2},{1,3},{2,0},{3,1},{4,6},{5,7},{6,4},{7,5},{8,10},{9,11},{10,... | collective-permute-start | bytes 786440 | tf_op jit(solution)/shard_map/ppermute | solution.py:21
  76.0 3.0 %collective-permute-start.11 = (f32[8,32,256]{2,1,0:T(8,128)S(1)}, f32[8,32,256]{2,1,0:T(8,128)S(1)}, u32[]{:S(2)}, u32[]{:S(2)}) collective-permute-start(f32[8,32,256]{2,1,0:T(8,128)S(1)} %get-tuple-element.9), channel_id=1, source_target_pairs={{0,4},{1,5},{2,6},{3,7},{4,0},{5,1},{6,2},{7,3},{8,12},{9,13},{10,... | collective-permute-start | bytes 786440 | tf_op jit(solution)/shard_map/ppermute | solution.py:21
  79.4 5.4 %collective-permute-start.13 = (f32[8,32,256]{2,1,0:T(8,128)S(1)}, f32[8,32,256]{2,1,0:T(8,128)S(1)}, u32[]{:S(2)}, u32[]{:S(2)}) collective-permute-start(f32[8,32,256]{2,1,0:T(8,128)S(1)} %get-tuple-element.7), channel_id=1, source_target_pairs={{0,6},{1,7},{2,4},{3,5},{4,2},{5,3},{6,0},{7,1},{8,14},{9,15},{10,... | collective-permute-start | bytes 786440 | tf_op jit(solution)/shard_map/ppermute | solution.py:21
  85.0 6.6 %collective-permute-done.9 = f32[8,32,256]{2,1,0:T(8,128)S(1)} collective-permute-done((f32[8,32,256]{2,1,0:T(8,128)S(1)}, f32[8,32,256]{2,1,0:T(8,128)S(1)}, u32[]{:S(2)}, u32[]{:S(2)}) %collective-permute-start.9) | collective-permute-done | bytes 262176 | tf_op jit(solution)/shard_map/ppermute | solution.py:21
  91.6 4.4 %collective-permute-start.14 = (f32[8,32,256]{2,1,0:T(8,128)S(1)}, f32[8,32,256]{2,1,0:T(8,128)S(1)}, u32[]{:S(2)}, u32[]{:S(2)}) collective-permute-start(f32[8,32,256]{2,1,0:T(8,128)S(1)} %get-tuple-element.6), channel_id=1, source_target_pairs={{0,7},{1,6},{2,5},{3,4},{4,3},{5,2},{6,1},{7,0},{8,15},{9,14},{10,... | collective-permute-start | bytes 786440 | tf_op jit(solution)/shard_map/ppermute | solution.py:21
  98.7 15.5 %collective-permute-done.12 = f32[8,32,256]{2,1,0:T(8,128)S(1)} collective-permute-done((f32[8,32,256]{2,1,0:T(8,128)S(1)}, f32[8,32,256]{2,1,0:T(8,128)S(1)}, u32[]{:S(2)}, u32[]{:S(2)}) %collective-permute-start.12) | collective-permute-done | bytes 262176 | tf_op jit(solution)/shard_map/ppermute | solution.py:21
  116.8 2.5 %copy.26 = f32[64,32,256]{2,1,0:T(8,128)} copy(f32[64,32,256]{2,0,1:T(8,128)S(1)} %convolution_bitcast_fusion) | data formatting | bytes 4194304 | tf_op jit(solution)/shard_map/cz,zne->cne/dot_general | solution.py:65
  119.3 14.6 %all-to-all-start = ((f32[64,32,256]{2,1,0:T(8,128)}), f32[64,32,256]{2,1,0:T(8,128)}, u32[]{:S(2)}, u32[]{:S(2)}) async-start(f32[64,32,256]{2,1,0:T(8,128)} %copy.26), calls=%async_computation | async-start | bytes 4194304 | tf_op jit(solution)/shard_map/all_to_all | solution.py:88
  134.6 46.3 %all-to-all-done = f32[64,32,256]{2,1,0:T(8,128)} async-done(((f32[64,32,256]{2,1,0:T(8,128)}), f32[64,32,256]{2,1,0:T(8,128)}, u32[]{:S(2)}, u32[]{:S(2)}) %all-to-all-start) | async-done | bytes 2097184 | tf_op jit(solution)/shard_map/all_to_all | solution.py:88
  180.9 3.2 %copy.29 = f32[8,8,4,8,256]{4,3,0,2,1:T(8,128)} copy(f32[8,8,4,8,256]{4,3,2,1,0:T(8,128)} %bitcast.6) | data formatting | bytes 4194304 | tf_op jit(solution)/shard_map/all_to_all | solution.py:88
  (49 shorter events, 18.9 us)
Async XLA Ops:
  0.6 114.1 %copy-start = (f32[64,64]{1,0:T(8,128)S(1)}, f32[64,64]{1,0:T(8,128)}, u32[]{:S(2)}) copy-start(f32[64,64]{1,0:T(8,128)} %param.13) | copy-start | bytes 49156
  0.6 24.6 %copy-start.1 = (f32[8,32,2048]{2,1,0:T(8,128)S(1)}, f32[8,32,2048]{2,1,0:T(8,128)}, u32[]{:S(2)}) copy-start(f32[8,32,2048]{2,1,0:T(8,128)} %param.7) | copy-start | bytes 6291460
  2.1 3.7 %collective-permute-start = (f32[8,1,2048]{2,1,0:T(1,128)S(1)}, f32[8,1,2048]{2,1,0:T(1,128)S(1)}, u32[]{:S(2)}, u32[]{:S(2)}) collective-permute-start(f32[8,1,2048]{2,1,0:T(1,128)S(1)} %get-tuple-element.16), channel_id=1, source_target_pairs={{0,8},{8,16},{16,24},{1,9},{9,17},{17,25},{2,10},{10,18},{18,26},{... | collective-permute-start | bytes 196616 | tf_op jit(solution)/shard_map/ppermute | solution.py:39
  4.5 5.3 %collective-permute-start.1 = (f32[8,1,2048]{2,1,0:T(1,128)S(1)}, f32[8,1,2048]{2,1,0:T(1,128)S(1)}, u32[]{:S(2)}, u32[]{:S(2)}) collective-permute-start(f32[8,1,2048]{2,1,0:T(1,128)S(1)} %get-tuple-element.17), channel_id=1, source_target_pairs={{8,0},{16,8},{24,16},{9,1},{17,9},{25,17},{10,2},{18,10},{26,18},{... | collective-permute-start | bytes 196616 | tf_op jit(solution)/shard_map/ppermute | solution.py:41
  10.9 9.3 %collective-permute-start.2 = (f32[1,34,2048]{2,1,0:T(8,128)S(1)}, f32[1,34,2048]{2,1,0:T(8,128)S(1)}, u32[]{:S(2)}, u32[]{:S(2)}) collective-permute-start(f32[1,34,2048]{2,1,0:T(8,128)S(1)} %get-tuple-element.4), channel_id=1, source_target_pairs={{0,1},{1,2},{2,3},{3,4},{4,5},{5,6},{6,7},{8,9},{9,10},{10,11},{11... | collective-permute-start | bytes 835592 | tf_op jit(solution)/shard_map/ppermute | solution.py:39
  14.3 14.0 %copy-start.2 = (f32[8,32,2048]{2,1,0:T(8,128)S(1)}, f32[8,32,2048]{2,1,0:T(8,128)}, u32[]{:S(2)}) copy-start(f32[8,32,2048]{2,1,0:T(8,128)} %param.8) | copy-start | bytes 6291460
  14.3 14.0 %copy-start.4 = (s32[8,32,2048]{2,1,0:T(8,128)S(1)}, s32[8,32,2048]{2,1,0:T(8,128)}, u32[]{:S(2)}) copy-start(s32[8,32,2048]{2,1,0:T(8,128)} %param.11) | copy-start | bytes 6291460
  14.3 14.0 %copy-start.6 = (f32[8,32,2048]{2,1,0:T(8,128)S(1)}, f32[8,32,2048]{2,1,0:T(8,128)}, u32[]{:S(2)}) copy-start(f32[8,32,2048]{2,1,0:T(8,128)} %param.10) | copy-start | bytes 6291460
  14.3 10.9 %collective-permute-start.3 = (f32[1,34,2048]{2,1,0:T(8,128)S(1)}, f32[1,34,2048]{2,1,0:T(8,128)S(1)}, u32[]{:S(2)}, u32[]{:S(2)}) collective-permute-start(f32[1,34,2048]{2,1,0:T(8,128)S(1)} %get-tuple-element.5), channel_id=1, source_target_pairs={{1,0},{2,1},{3,2},{4,3},{5,4},{6,5},{7,6},{9,8},{10,9},{11,10},{12... | collective-permute-start | bytes 835592 | tf_op jit(solution)/shard_map/ppermute | solution.py:41
  32.7 7.5 %collective-permute-start.4 = (f32[8,1,2048]{2,1,0:T(1,128)S(1)}, f32[8,1,2048]{2,1,0:T(1,128)S(1)}, u32[]{:S(2)}, u32[]{:S(2)}) collective-permute-start(f32[8,1,2048]{2,1,0:T(1,128)S(1)} %get-tuple-element.14), channel_id=1, source_target_pairs={{0,8},{8,16},{16,24},{1,9},{9,17},{17,25},{2,10},{10,18},{18,26},{... | collective-permute-start | bytes 196616 | tf_op jit(solution)/shard_map/ppermute | solution.py:39
  38.9 3.1 %collective-permute-start.5 = (f32[8,1,2048]{2,1,0:T(1,128)S(1)}, f32[8,1,2048]{2,1,0:T(1,128)S(1)}, u32[]{:S(2)}, u32[]{:S(2)}) collective-permute-start(f32[8,1,2048]{2,1,0:T(1,128)S(1)} %get-tuple-element.15), channel_id=1, source_target_pairs={{8,0},{16,8},{24,16},{9,1},{17,9},{25,17},{10,2},{18,10},{26,18},{... | collective-permute-start | bytes 196616 | tf_op jit(solution)/shard_map/ppermute | solution.py:41
  42.9 10.9 %collective-permute-start.6 = (f32[1,34,2048]{2,1,0:T(8,128)}, f32[1,34,2048]{2,1,0:T(8,128)S(1)}, u32[]{:S(2)}, u32[]{:S(2)}) collective-permute-start(f32[1,34,2048]{2,1,0:T(8,128)} %get-tuple-element.2), channel_id=1, source_target_pairs={{0,1},{1,2},{2,3},{3,4},{4,5},{5,6},{6,7},{8,9},{9,10},{10,11},{11... | collective-permute-start | bytes 835592 | tf_op jit(solution)/shard_map/ppermute | solution.py:39
  47.0 11.5 %collective-permute-start.7 = (f32[1,34,2048]{2,1,0:T(8,128)S(1)}, f32[1,34,2048]{2,1,0:T(8,128)S(1)}, u32[]{:S(2)}, u32[]{:S(2)}) collective-permute-start(f32[1,34,2048]{2,1,0:T(8,128)S(1)} %get-tuple-element.3), channel_id=1, source_target_pairs={{1,0},{2,1},{3,2},{4,3},{5,4},{6,5},{7,6},{9,8},{10,9},{11,10},{12... | collective-permute-start | bytes 835592 | tf_op jit(solution)/shard_map/ppermute | solution.py:41
  48.5 13.2 %copy-start.3 = (f32[8,32,2048]{2,1,0:T(8,128)S(1)}, f32[8,32,2048]{2,1,0:T(8,128)}, u32[]{:S(2)}) copy-start(f32[8,32,2048]{2,1,0:T(8,128)} %param.8) | copy-start | bytes 6291460
  48.5 13.2 %copy-start.5 = (s32[8,32,2048]{2,1,0:T(8,128)S(1)}, s32[8,32,2048]{2,1,0:T(8,128)}, u32[]{:S(2)}) copy-start(s32[8,32,2048]{2,1,0:T(8,128)} %param.11) | copy-start | bytes 6291460
  66.2 13.2 %collective-permute-start.8 = (f32[8,32,256]{2,1,0:T(8,128)S(1)}, f32[8,32,256]{2,1,0:T(8,128)S(1)}, u32[]{:S(2)}, u32[]{:S(2)}) collective-permute-start(f32[8,32,256]{2,1,0:T(8,128)S(1)} %get-tuple-element.12), channel_id=1, source_target_pairs={{0,1},{1,0},{2,3},{3,2},{4,5},{5,4},{6,7},{7,6},{8,9},{9,8},{10,11... | collective-permute-start | bytes 786440 | tf_op jit(solution)/shard_map/ppermute | solution.py:21
  71.0 20.6 %collective-permute-start.9 = (f32[8,32,256]{2,1,0:T(8,128)S(1)}, f32[8,32,256]{2,1,0:T(8,128)S(1)}, u32[]{:S(2)}, u32[]{:S(2)}) collective-permute-start(f32[8,32,256]{2,1,0:T(8,128)S(1)} %get-tuple-element.11), channel_id=1, source_target_pairs={{0,2},{1,3},{2,0},{3,1},{4,6},{5,7},{6,4},{7,5},{8,10},{9,11},{10,... | collective-permute-start | bytes 786440 | tf_op jit(solution)/shard_map/ppermute | solution.py:21
  74.6 23.7 %collective-permute-start.10 = (f32[8,32,256]{2,1,0:T(8,128)S(1)}, f32[8,32,256]{2,1,0:T(8,128)S(1)}, u32[]{:S(2)}, u32[]{:S(2)}) collective-permute-start(f32[8,32,256]{2,1,0:T(8,128)S(1)} %get-tuple-element.10), channel_id=1, source_target_pairs={{0,3},{1,2},{2,1},{3,0},{4,7},{5,6},{6,5},{7,4},{8,11},{9,10},{10,... | collective-permute-start | bytes 786440 | tf_op jit(solution)/shard_map/ppermute | solution.py:21
  76.0 22.5 %collective-permute-start.11 = (f32[8,32,256]{2,1,0:T(8,128)S(1)}, f32[8,32,256]{2,1,0:T(8,128)S(1)}, u32[]{:S(2)}, u32[]{:S(2)}) collective-permute-start(f32[8,32,256]{2,1,0:T(8,128)S(1)} %get-tuple-element.9), channel_id=1, source_target_pairs={{0,4},{1,5},{2,6},{3,7},{4,0},{5,1},{6,2},{7,3},{8,12},{9,13},{10,... | collective-permute-start | bytes 786440 | tf_op jit(solution)/shard_map/ppermute | solution.py:21
  79.0 35.2 %collective-permute-start.12 = (f32[8,32,256]{2,1,0:T(8,128)S(1)}, f32[8,32,256]{2,1,0:T(8,128)S(1)}, u32[]{:S(2)}, u32[]{:S(2)}) collective-permute-start(f32[8,32,256]{2,1,0:T(8,128)S(1)} %get-tuple-element.8), channel_id=1, source_target_pairs={{0,5},{1,4},{2,7},{3,6},{4,1},{5,0},{6,3},{7,2},{8,13},{9,12},{10,... | collective-permute-start | bytes 786440 | tf_op jit(solution)/shard_map/ppermute | solution.py:21
  79.4 34.9 %collective-permute-start.13 = (f32[8,32,256]{2,1,0:T(8,128)S(1)}, f32[8,32,256]{2,1,0:T(8,128)S(1)}, u32[]{:S(2)}, u32[]{:S(2)}) collective-permute-start(f32[8,32,256]{2,1,0:T(8,128)S(1)} %get-tuple-element.7), channel_id=1, source_target_pairs={{0,6},{1,7},{2,4},{3,5},{4,2},{5,3},{6,0},{7,1},{8,14},{9,15},{10,... | collective-permute-start | bytes 786440 | tf_op jit(solution)/shard_map/ppermute | solution.py:21
  91.6 22.9 %collective-permute-start.14 = (f32[8,32,256]{2,1,0:T(8,128)S(1)}, f32[8,32,256]{2,1,0:T(8,128)S(1)}, u32[]{:S(2)}, u32[]{:S(2)}) collective-permute-start(f32[8,32,256]{2,1,0:T(8,128)S(1)} %get-tuple-element.6), channel_id=1, source_target_pairs={{0,7},{1,6},{2,5},{3,4},{4,3},{5,2},{6,1},{7,0},{8,15},{9,14},{10,... | collective-permute-start | bytes 786440 | tf_op jit(solution)/shard_map/ppermute | solution.py:21
  119.3 14.6 %copy-start.8 = (s32[32,256]{1,0:T(8,128)S(1)}, s32[32,256]{1,0:T(8,128)}, u32[]{:S(2)}) copy-start(s32[32,256]{1,0:T(8,128)} %param.12) | copy-start | bytes 98308
  119.3 61.5 %all-to-all-start = ((f32[64,32,256]{2,1,0:T(8,128)}), f32[64,32,256]{2,1,0:T(8,128)}, u32[]{:S(2)}, u32[]{:S(2)}) async-start(f32[64,32,256]{2,1,0:T(8,128)} %copy.26), calls=%async_computation | async-start | bytes 4194304 | tf_op jit(solution)/shard_map/all_to_all | solution.py:88
  (1 other events, 13.2 us)
